TPU v7x, 32 devices: a whole 2x2x4 slice. The times are simulated.
32 devices in a mesh: groups: 2 (over x), gx: 16 (over z, y, core).
Axes of the slice: x: 2, y: 2, z: 4, core: 2. Of those that a mesh axis runs over, the one named last changes fastest.
Arguments:
- features: bfloat16 [64, 98304], P(None, ('groups', 'gx')), parts along dimension 1, may hold values from -6 to 6
- cotangent: bfloat16 [64, 98304], P(None, ('groups', 'gx')), parts along dimension 1, may hold values from -6 to 6
- weights: bfloat16 [27, 64, 64], replicated, may hold values from -0.15625 to 0.15625
- kernel_map: int32 [27, 98304], P(None, ('groups', 'gx')), parts along dimension 1, may hold values from 0 to 5120, as said below
- interior_bricks: int32 [32], P(('groups', 'gx')), parts along dimension 0, may hold values from 0 to 8, as said below
Outputs:
- output: bfloat16 [64, 98304], P(None, ('groups', 'gx')), parts along dimension 1
- grad_features: bfloat16 [64, 98304], P(None, ('groups', 'gx')), parts along dimension 1
- grad_weights: float32 [54, 64, 64], P('groups'), parts along dimension 0
There are 2 independent parts, one for each index of `groups`. A program takes and returns all parts, laid end to end along the dimension named above; an argument that names none is the same for every part. Nothing has to cross between parts.
Inputs may be any that keep to these rules, and one draw needn't show every extreme that they name: Offsets are ordered k = 9 (dx + 1) + 3 (dy + 1) + (dz + 1). A voxel's sources lie on its own device or in the outermost 8 bricks of an adjacent device; a value of 5120 means no source. The maps are symmetric: where kernel_map[k, v] names voxel w, kernel_map[26 - k, w] names v. Voxels that are not live have no sources and are no one's source. `interior_bricks`: the occupied inner bricks of a device fill the slots right after its first 8; the other inner slots are empty.
All inputs are finite; a program needn't handle non-finite values.
Results may differ from a plain program's by a relative error of at most 0.0025.
Values may be sent and summed in bfloat16 or wider, within the bound.
A program may use at most 128 MiB of HBM per device.

v0:
```python
import jax
import jax.numpy as jnp
from jax import lax
from jax.sharding import PartitionSpec as P

RB = 8


def extended(cells, sides, width):
    for axis, dim in sides:
        count = lax.axis_size(axis)
        ends = count - 1
        head = lax.slice_in_dim(cells, 0, width, axis=dim)
        tail = lax.slice_in_dim(cells, cells.shape[dim] - width, cells.shape[dim], axis=dim)
        cells = jnp.concatenate(
            [
                lax.ppermute(tail, axis, [(i, (i + 1) % count) for i in range(ends)]),
                cells,
                lax.ppermute(head, axis, [((i + 1) % count, i) for i in range(ends)]),
            ],
            axis=dim,
        )
    return cells


def shifted(block, axis, distance):
    devices = range(lax.axis_size(axis))
    route = [(i - distance, i) for i in devices if i - distance in devices]
    return lax.ppermute(block, axis, route)


def per_device(features, cotangent, weights, kernel_map, interior_bricks):
    channels = features.shape[0]
    own_len = features.shape[1]
    rim_len = RB * 128
    layer_total = own_len // rim_len
    bricks_own = own_len // 128
    filled = interior_bricks[0]
    slot_ids = jnp.arange(own_len, dtype=jnp.int32) // 128
    live = (slot_ids < RB) | (slot_ids >= bricks_own - RB) | (slot_ids - RB < filled)
    upstream = jnp.where(live[None, :], cotangent, jnp.zeros_like(cotangent))
    w_forward = jnp.transpose(weights, (1, 2, 0)).reshape(channels, channels * 27)
    feature_ext = extended(features, (("gx", 1),), rim_len)
    grad_buffer = jnp.zeros((channels, own_len + 2 * rim_len), jnp.float32)

    def visit_layer(turn, state_now):
        output, grad_features, weight_sum, grad_buffer = state_now
        begin = turn * rim_len
        indices = lax.dynamic_slice_in_dim(kernel_map, begin, rim_len, 1)
        picked = jnp.take(feature_ext, indices, axis=1, mode="fill", fill_value=0).reshape(
            channels * 27, rim_len
        )
        mask_part = lax.dynamic_slice_in_dim(live, begin, rim_len, 0)[None, :]
        result = jnp.dot(w_forward, picked, preferred_element_type=jnp.float32)
        result = jnp.where(mask_part, result, 0.0).astype(jnp.bfloat16)
        output = lax.dynamic_update_slice_in_dim(output, result, begin, 1)
        upstream_part = lax.dynamic_slice_in_dim(upstream, begin, rim_len, 1)
        weight_sum = weight_sum + lax.dot_general(
            upstream_part, picked, (((1,), (1,)), ((), ())), preferred_element_type=jnp.float32
        )
        spread = lax.dot_general(
            w_forward, upstream_part, (((0,), (0,)), ((), ())), preferred_element_type=jnp.float32
        )
        grad_buffer = grad_buffer.at[:, indices].add(
            spread.reshape(channels, 27, rim_len), mode="drop"
        )
        return (output, grad_features, weight_sum, grad_buffer)

    initial = (
        jnp.zeros((channels, own_len), jnp.bfloat16),
        jnp.zeros((channels, own_len), jnp.bfloat16),
        jnp.zeros((channels, channels * 27), jnp.float32),
        grad_buffer,
    )
    output, grad_features, weight_sum, grad_buffer = lax.fori_loop(
        0, layer_total, visit_layer, initial
    )
    summed = lax.psum(weight_sum, "gx")
    factor = float(lax.axis_size("gx") * own_len) ** (-0.5)
    grad_weights = jnp.transpose((summed * factor).reshape(channels, channels, 27), (2, 0, 1))
    left_part = grad_buffer[:, :rim_len]
    right_part = grad_buffer[:, own_len + rim_len :]
    from_right = shifted(left_part.astype(jnp.bfloat16), "gx", -1).astype(left_part.dtype)
    from_left = shifted(right_part.astype(jnp.bfloat16), "gx", 1).astype(right_part.dtype)
    middle = grad_buffer[:, rim_len : own_len + rim_len]
    middle = middle.at[:, :rim_len].add(from_left)
    middle = middle.at[:, own_len - rim_len :].add(from_right)
    grad_features = jnp.where(live[None, :], middle, 0.0).astype(jnp.bfloat16)
    return (output, grad_features, grad_weights)


def solution(mesh):
    placed = (
        P(None, ("groups", "gx")),
        P(None, ("groups", "gx")),
        P(),
        P(None, ("groups", "gx")),
        P(("groups", "gx")),
    )
    return jax.shard_map(
        per_device,
        mesh=mesh,
        in_specs=placed,
        out_specs=(P(None, ("groups", "gx")), P(None, ("groups", "gx")), P("groups", None, None)),
        check_vma=False,
    )
```

profile of v0, /device:TPU:0, one launch (start us, length us, event | category | flops | bytes accessed | tf_op | source)
XLA Modules:
  0.0 1012.2 jit_solution(18138434684973174457)
XLA Ops:
  9.3 2.4 collective-permute-start
  21.1 876.3 %while.20 = (s32[]{:T(128)}, bf16[64,3072]{1,0:T(8,128)(2,1)}, f32[64,1728]{1,0:T(8,128)S(1)}, f32[64,5120]{0,1:T(8,128)S(1)}, pred[3072]{0:T(1024)(128)(4,1)S(1...) while((s32[]{:T(128)}, bf16[64,3072]{1,0:T(8,128)(2,1)}, ...), condition=%wide.region_2.3_spmd.clone, body=%wide.region_0.2_spmd.clone.sunk | while | flops 683561984 | bytes 108942592 | solution.py:75
  22.7 94.5 %gather_fusion = bf16[27648,64]{1,0:T(8,128)(2,1)} fusion(bf16[64,5120]{0,1:T(8,128)(2,1)} %get-tuple-element.355, s32[27648]{0:T(1024)S(1)} %broadcast_clamp_fusion.2), kind=kCustom, calls=%fused_computation.clone.clone.1 | custom fusion | bytes 7188480 | tf_op jit(solution)/shard_map/while/body/eval_jaxpr/jit(_take)/gather | solution.py:50
  117.3 9.9 copy.45
  127.1 4.5 select_bitcast_fusion.2
  131.7 5.0 select_n.105
  136.7 3.4 convolution_add_fusion.2
  141.6 5.0 convolution_bitcast_fusion.2
  146.5 6.8 reshape.146
  153.3 11.7 %copy.46 = f32[27,1024,64]{2,1,0:T(8,128)} copy(f32[27,1024,64]{1,0,2:T(8,128)} %bitcast.42) | data formatting | bytes 14155776 | tf_op jit(solution)/shard_map/while/body/eval_jaxpr/reshape | solution.py:65
  165.0 148.2 %scatter_fusion = f32[64,5120]{0,1:T(8,128)S(1)} fusion(f32[64,5120]{0,1:T(8,128)S(1)} %get-tuple-element.339, s32[27648]{0:T(1024)S(1)} %reshape.145, f32[27648,64]{1,0:T(8,128)} %bitcast.41), kind=kCustom, calls=%fused_computation.1.clone.clone.1 | custom fusion | flops 1769472 | bytes 21344256 | tf_op jit(solution)/shard_map/while/body/eval_jaxpr/scatter-add | solution.py:64
  314.8 94.5 %gather_fusion = bf16[27648,64]{1,0:T(8,128)(2,1)} fusion(bf16[64,5120]{0,1:T(8,128)(2,1)} %get-tuple-element.355, s32[27648]{0:T(1024)S(1)} %broadcast_clamp_fusion.2), kind=kCustom, calls=%fused_computation.clone.clone.1 | custom fusion | bytes 7188480 | tf_op jit(solution)/shard_map/while/body/eval_jaxpr/jit(_take)/gather | solution.py:50
  409.4 9.9 copy.45
  419.2 4.5 select_bitcast_fusion.2
  423.8 5.0 select_n.105
  428.8 3.5 convolution_add_fusion.2
  433.7 5.0 convolution_bitcast_fusion.2
  438.6 6.8 reshape.146
  445.4 11.7 %copy.46 = f32[27,1024,64]{2,1,0:T(8,128)} copy(f32[27,1024,64]{1,0,2:T(8,128)} %bitcast.42) | data formatting | bytes 14155776 | tf_op jit(solution)/shard_map/while/body/eval_jaxpr/reshape | solution.py:65
  457.2 148.2 %scatter_fusion = f32[64,5120]{0,1:T(8,128)S(1)} fusion(f32[64,5120]{0,1:T(8,128)S(1)} %get-tuple-element.339, s32[27648]{0:T(1024)S(1)} %reshape.145, f32[27648,64]{1,0:T(8,128)} %bitcast.41), kind=kCustom, calls=%fused_computation.1.clone.clone.1 | custom fusion | flops 1769472 | bytes 21344256 | tf_op jit(solution)/shard_map/while/body/eval_jaxpr/scatter-add | solution.py:64
  607.0 94.5 %gather_fusion = bf16[27648,64]{1,0:T(8,128)(2,1)} fusion(bf16[64,5120]{0,1:T(8,128)(2,1)} %get-tuple-element.355, s32[27648]{0:T(1024)S(1)} %broadcast_clamp_fusion.2), kind=kCustom, calls=%fused_computation.clone.clone.1 | custom fusion | bytes 7188480 | tf_op jit(solution)/shard_map/while/body/eval_jaxpr/jit(_take)/gather | solution.py:50
  701.5 9.9 copy.45
  711.3 4.5 select_bitcast_fusion.2
  715.9 5.0 select_n.105
  720.9 3.5 convolution_add_fusion.2
  725.8 5.0 convolution_bitcast_fusion.2
  730.7 6.8 reshape.146
  737.5 11.7 %copy.46 = f32[27,1024,64]{2,1,0:T(8,128)} copy(f32[27,1024,64]{1,0,2:T(8,128)} %bitcast.42) | data formatting | bytes 14155776 | tf_op jit(solution)/shard_map/while/body/eval_jaxpr/reshape | solution.py:65
  749.3 148.2 %scatter_fusion = f32[64,5120]{0,1:T(8,128)S(1)} fusion(f32[64,5120]{0,1:T(8,128)S(1)} %get-tuple-element.339, s32[27648]{0:T(1024)S(1)} %reshape.145, f32[27648,64]{1,0:T(8,128)} %bitcast.41), kind=kCustom, calls=%fused_computation.1.clone.clone.1 | custom fusion | flops 1769472 | bytes 21344256 | tf_op jit(solution)/shard_map/while/body/eval_jaxpr/scatter-add | solution.py:64
  900.9 5.1 collective-permute-start.2
  908.7 2.4 collective-permute-done.3
  912.0 90.4 %all-reduce.2.cloned.1.call-done = f32[64,1728]{1,0:T(8,128)} async-done(((f32[64,1728]{1,0:T(8,128)}), f32[64,1728]{1,0:T(8,128)}) %all-reduce.2.cloned.1.call-update) | async-done | bytes 442384 | tf_op jit(solution)/shard_map/psum | solution.py:78
  (61 shorter events, 29.8 us)
Async XLA Ops:
  7.2 995.3 %all-reduce.2.cloned.1.call-start = ((), (), s32[]{:S(2)}) async-start(), calls=%async_computation | async-start | bytes 917504 | tf_op jit(solution)/shard_map/psum | solution.py:78
  9.3 9.5 collective-permute-start
  11.7 7.1 collective-permute-start.1
  117.3 9.9 copy-start.3
  136.7 3.5 copy-start
  409.4 9.9 copy-start.3
  428.8 3.5 copy-start
  701.5 9.9 copy-start.3
  720.9 3.5 copy-start
  897.4 9.2 copy-start.1
  899.3 8.7 copy-start.2
  899.3 8.7 slice-start
  900.9 7.1 collective-permute-start.2
  906.7 4.5 collective-permute-start.3
Sparse Core Ops, SparseCore 0:
  908.1 94.2 all-reduce.1
where the time goes:
time: 1010 us
  other arithmetic  471 us (47%)
  local copies, waits for them, and re-layouts  394 us (39%)
  waiting for transfers between devices  92.9 us (9%)
  matrix products  29.4 us (3%)
  between operations  14.8 us (1%)
  starting transfers between devices  10.1 us (1%)
    scatter-add x3, other arithmetic, visit_layer(): grad_buffer.at[:, indices]  444 us
    gather x6, local copies, waits for them, and re-layouts, visit_layer(): jnp.take(feature_ext, indices, axis=1, mode='fill', fill_value=0)  313 us
    psum x1, waiting for transfers between devices, per_device(): summed = lax.psum(weight_sum, 'gx')  90.4 us
    reshape x6, local copies, waits for them, and re-layouts, visit_layer(): spread.reshape(channels, 27, rim_len)  55.6 us
  transfers between devices with their start and end apart: 5, of which 2 were waited for; matrix products, arithmetic and copies ran while one was open for 1% of the time, Pallas kernels for 0%

commit v1 on v0

v1 whole, which is shorter than its diff:
```python
import functools

import jax
import jax.numpy as jnp
from jax import lax
from jax.experimental import pallas as pl
from jax.experimental.pallas import tpu as pltpu
from jax.sharding import PartitionSpec as P

RB = 8
BRICK = 128
ROWS = 256


def gather_kernel(
    taps, channels, own_len, factor,
    flags, index, filled,
    feat, cot, left, right, stack,
    out_ref, gf_ref, gw_ref,
    picked, table, block, ups, compact, result,
):
    rim_len = RB * BRICK
    wide = 2 * channels
    none = own_len + 2 * rim_len
    bricks = own_len // BRICK

    def fill_table(start, tile):
        table[pl.ds(start, BRICK), :] = tile.astype(jnp.float32).T

    for b in range(RB):
        cols = slice(b * BRICK, (b + 1) * BRICK)
        fill_table(b * BRICK, left[:, cols])
        fill_table(rim_len + own_len + b * BRICK, right[:, cols])
    for b in range(bricks):
        cols = slice(b * BRICK, (b + 1) * BRICK)
        up = cot[:, cols].astype(jnp.float32)
        if RB <= b < bricks - RB:
            up = jnp.where(b - RB < filled[0], up, 0.0)
        own = jnp.concatenate([feat[:, cols].astype(jnp.float32), up], axis=0)
        fill_table(rim_len + b * BRICK, own)
    table[pl.ds(none, 8), :] = jnp.zeros((8, wide), jnp.float32)
    result[...] = jnp.zeros_like(result)
    gw_ref[...] = jnp.zeros_like(gw_ref)

    def note(step, count):
        for j in range(16):
            voxel = step * 16 + j
            picked[count] = voxel
            count = count + flags[voxel]
        return count

    count = lax.fori_loop(0, own_len // 16, note, 0)

    def pad(i, _):
        picked[count + i] = 0
        return _

    lax.fori_loop(0, ROWS, pad, 0)

    def visit(blk, _):
        base = blk * ROWS

        def fetch(step, _):
            for j in range(8):
                voxel = picked[base + step * 8 + j]
                ups[step, j : j + 1, :] = table[pl.ds(voxel + rim_len, 1), :]
                for k in range(taps):
                    source = index[k * own_len + voxel]
                    block[step, j : j + 1, k * wide : (k + 1) * wide] = table[pl.ds(source, 1), :]
            return _

        lax.fori_loop(0, ROWS // 8, fetch, 0)
        up = ups[...].reshape(ROWS, wide)
        row = lax.broadcasted_iota(jnp.int32, (ROWS, wide), 0)
        up = jnp.where(row + base < count, up, 0.0)
        up = up.T[channels:].astype(jnp.bfloat16)
        total = jnp.zeros((ROWS, wide), jnp.float32)
        for k in range(0, taps, 2):
            many = min(2, taps - k)
            cols = slice(k * wide, (k + many) * wide)
            part = block[:, :, cols].reshape(ROWS, many * wide).astype(jnp.bfloat16)
            total += jnp.dot(part, stack[cols, :], preferred_element_type=jnp.float32)
            grad = jnp.dot(up, part, preferred_element_type=jnp.float32)
            for m in range(many):
                gw_ref[k + m] += grad[:, m * wide : m * wide + channels]
        compact[pl.ds(pl.multiple_of(base, ROWS), ROWS), :] = total
        return _

    lax.fori_loop(0, (count + ROWS - 1) // ROWS, visit, 0)
    gw_ref[...] = gw_ref[...] * factor

    def place(step, _):
        for j in range(8):
            at = step * 8 + j
            result[pl.ds(picked[at], 1), :] = compact[pl.ds(at, 1), :]
        return _

    lax.fori_loop(0, count // 8, place, 0)

    def place_one(at, _):
        result[pl.ds(picked[at], 1), :] = compact[pl.ds(at, 1), :]
        return _

    lax.fori_loop(count // 8 * 8, count, place_one, 0)

    for b in range(bricks):
        cols = slice(b * BRICK, (b + 1) * BRICK)
        both = result[cols, :].T
        if RB <= b < bricks - RB:
            both = jnp.where(b - RB < filled[0], both, 0.0)
        out_ref[:, cols] = both[:channels].astype(jnp.bfloat16)
        gf_ref[:, cols] = both[channels:].astype(jnp.bfloat16)


def per_device(features, cotangent, weights, kernel_map, interior_bricks):
    channels, own_len = features.shape
    taps = weights.shape[0]
    rim_len = RB * BRICK
    wide = 2 * channels
    count = lax.axis_size("gx")
    none = own_len + 2 * rim_len
    factor = float(count * own_len) ** (-0.5)

    tail = jnp.concatenate([features[:, own_len - rim_len :], cotangent[:, own_len - rim_len :]], 0)
    head = jnp.concatenate([features[:, :rim_len], cotangent[:, :rim_len]], 0)
    left = lax.ppermute(tail, "gx", [(i, i + 1) for i in range(count - 1)])
    right = lax.ppermute(head, "gx", [(i + 1, i) for i in range(count - 1)])
    flags = jnp.any(kernel_map != none, axis=0).astype(jnp.int32)
    zero = jnp.zeros_like(weights)
    stack = jnp.concatenate(
        [
            jnp.concatenate([jnp.transpose(weights, (0, 2, 1)), zero], 2),
            jnp.concatenate([zero, weights[::-1]], 2),
        ],
        1,
    ).reshape(taps * wide, wide)
    smem = pl.BlockSpec(memory_space=pltpu.SMEM)
    vmem = pl.BlockSpec(memory_space=pltpu.VMEM)
    output, grad_features, partial = pl.pallas_call(
        functools.partial(gather_kernel, taps, channels, own_len, factor),
        out_shape=(
            jax.ShapeDtypeStruct((channels, own_len), jnp.bfloat16),
            jax.ShapeDtypeStruct((channels, own_len), jnp.bfloat16),
            jax.ShapeDtypeStruct((taps, channels, channels), jnp.float32),
        ),
        in_specs=[smem] * 3 + [vmem] * 5,
        out_specs=(vmem,) * 3,
        scratch_shapes=[
            pltpu.SMEM((own_len + ROWS,), jnp.int32),
            pltpu.VMEM((none + 8, wide), jnp.float32),
            pltpu.VMEM((ROWS // 8, 8, taps * wide), jnp.float32),
            pltpu.VMEM((ROWS // 8, 8, wide), jnp.float32),
            pltpu.VMEM((own_len, wide), jnp.float32),
            pltpu.VMEM((own_len, wide), jnp.float32),
        ],
        compiler_params=pltpu.CompilerParams(vmem_limit_bytes=48 * 1024 * 1024),
    )(flags, kernel_map.reshape(-1), interior_bricks, features, cotangent, left, right, stack)
    grad_weights = lax.psum(partial, "gx")
    return output, grad_features, grad_weights


def solution(mesh):
    placed = (
        P(None, ("groups", "gx")),
        P(None, ("groups", "gx")),
        P(),
        P(None, ("groups", "gx")),
        P(("groups", "gx")),
    )
    return jax.shard_map(
        per_device,
        mesh=mesh,
        in_specs=placed,
        out_specs=(P(None, ("groups", "gx")), P(None, ("groups", "gx")), P("groups", None, None)),
        check_vma=False,
    )
```

time: 1010 us -> 185 us (0.18)
  other arithmetic: 471 us -> 0.36 us
  local copies, waits for them, and re-layouts: 394 us -> 3.74 us
  Pallas kernels: 0 us -> 49.1 us
  matrix products: 29.4 us -> 0 us
  waiting for transfers between devices: 92.9 us -> 112 us
    scatter-add x5 -> x0, other arithmetic: 445 us -> none  [the longest x3 444 us: visit_layer(): grad_buffer.at[:, indices]]
    gather x6 -> x0, local copies, waits for them, and re-layouts: 313 us -> none  [visit_layer(): jnp.take(feature_ext, indices, axis=1, mode='fill', fill_value=0)]
    reshape x7 -> x1, local copies, waits for them, and re-layouts: 55.7 us -> 0.05 us  [per_device(): kernel_map.reshape(-1)]
    pallas_call x0 -> x1, Pallas kernels: none -> 49.1 us  [per_device(): pl.pallas_call(functools.partial(gather_kernel, taps, channels, own_len,...]
    dot_general x9 -> x0, matrix products: 29.4 us -> none  [the longest x3 14.9 us: visit_layer(): lax.dot_general(w_forward, upstream_part, (((0,), (0,)), ((), ())), prefe...]
    psum x1, waiting for transfers between devices: 90.4 us -> 109 us  [per_device(): grad_weights = lax.psum(partial, 'gx')]
    select_n x4 -> x0, other arithmetic: 15.4 us -> none  [the longest x3 13.6 us: visit_layer(): jnp.take(feature_ext, indices, axis=1, mode='fill', fill_value=0)]
    select_n x3 -> x0, local copies, waits for them, and re-layouts: 15 us -> none  [visit_layer(): jnp.take(feature_ext, indices, axis=1, mode='fill', fill_value=0)]
  transfers between devices with their start and end apart: 5 -> 3, of which waited for: 2 -> 2; matrix products, arithmetic and copies ran while one was open for 1% -> 0% of each run, Pallas kernels for 0% -> 0%
where the time goes in v1:
time: 185 us; the launch traced here: 184 us
  waiting for transfers between devices  112 us (61%)
  Pallas kernels  49.1 us (27%)
  between operations  14.8 us (8%)
  starting transfers between devices  3.83 us (2%)
  local copies, waits for them, and re-layouts  3.74 us (2%)
    psum x1, waiting for transfers between devices, per_device(): grad_weights = lax.psum(partial, 'gx')  109 us
    pallas_call x1, Pallas kernels, per_device(): pl.pallas_call(functools.partial(gather_kernel, taps, channels, own_len,...  49.1 us
  transfers between devices with their start and end apart: 3, of which 2 were waited for; matrix products, arithmetic and copies ran while one was open for 0% of the time, Pallas kernels for 0%

profile of v1, /device:TPU:0, one launch (start us, length us, event | category | flops | bytes accessed | tf_op | source)
XLA Modules:
  0.0 183.5 jit_solution(3621063784507589492)
XLA Ops:
  7.2 0.0 copy-start.2
  7.2 0.0 all-reduce.4.cloned.1.call-start
  7.2 1.2 fusion.3
  8.4 2.4 %collective-permute-start = (bf16[128,1024]{1,0:T(8,128)(2,1)S(1)}, bf16[128,1024]{1,0:T(8,128)(2,1)S(1)}, u32[]{:S(2)}, u32[]{:S(2)}) collective-permute-start(bf16[128,1024]{1,0:T(8,128)(2,1)S(1)} %pad_maximum_fusion), channel_id=1, source_target_pairs={{0,1},{1,2},{2,3},{3,4},{4,5},{5,6},{6,7},{7,8},{8,9},{9,10},{10,1... | collective-permute-start | bytes 786440 | tf_op jit(solution)/shard_map/ppermute | solution.py:126
  10.8 0.0 copy-start.3
  10.8 1.4 collective-permute-start.1
  12.3 0.0 copy-done.2
  12.3 0.3 copy.8
  13.3 0.0 copy-done.3
  13.3 0.1 reshape.12.index
  13.3 0.1 compare_reduce_fusion
  13.4 0.0 copy-start
  13.4 0.0 copy-start.1
  13.4 0.3 fusion.2
  13.7 0.0 collective-permute-done.left
  13.7 2.8 %collective-permute-done.1.right = bf16[128,1024]{1,0:T(8,128)(2,1)S(1)} collective-permute-done((bf16[128,1024]{1,0:T(8,128)(2,1)S(1)}, bf16[128,1024]{1,0:T(8,128)(2,1)S(1)}, u32[]{:S(2)}, u32[]{:S(2)}) %collective-permute-start.1) | collective-permute-done | bytes 262176 | tf_op jit(solution)/shard_map/ppermute | solution.py:127
  16.5 0.0 copy-done
  16.5 0.0 copy-done.1
  16.5 49.1 %shard_map.76 = (bf16[64,3072]{1,0:T(8,128)(2,1)}, bf16[64,3072]{1,0:T(8,128)(2,1)}, f32[27,64,64]{2,1,0:T(8,128)}) custom-call(s32[3072]{0:T(1024)S(1)} %convert_element_type.3.flags, s32[82944]{0:T(1024)S(1)} %reshape.12.index, s32[1]{0:T(128)S(6)} %copy.10.filled, bf16[64,3072]{1,0:T(8,128)(2,1)S(1)} %copy-done, bf16[64,3072]{1,0:T(8,128)(2,1)S(1)} %copy-done.1, ...), custom_call_target="tpu_custom_call" | custom-call | tf_op jit(solution)/shard_map/pallas_call | solution.py:139
  65.6 0.0 all-reduce.4.cloned.1.call-update
  65.6 108.9 %all-reduce.4.cloned.1.call-done = f32[27,64,64]{2,1,0:T(8,128)} async-done(((f32[27,64,64]{2,1,0:T(8,128)}), f32[27,64,64]{2,1,0:T(8,128)}) %all-reduce.4.cloned.1.call-update) | async-done | bytes 442384 | tf_op jit(solution)/shard_map/psum | solution.py:158
  174.5 2.2 %copy.11 = f32[27,64,64]{2,1,0:T(8,128)} copy(f32[27,64,64]{2,1,0:T(8,128)} %all-reduce.4.cloned.1.call-done) | data formatting | bytes 884736
  (4 shorter events, 0.1 us)
Async XLA Ops:
  7.2 5.1 %copy-start.2 = (bf16[27,64,64]{2,1,0:T(8,128)(2,1)S(1)}, bf16[27,64,64]{2,1,0:T(8,128)(2,1)}, u32[]{:S(2)}) copy-start(bf16[27,64,64]{2,1,0:T(8,128)(2,1)} %param.7) | copy-start | bytes 663556
  7.2 167.3 %all-reduce.4.cloned.1.call-start = ((), (), s32[]{:S(2)}) async-start(), calls=%async_computation | async-start | bytes 1769472 | tf_op jit(solution)/shard_map/psum | solution.py:158
  8.4 5.3 %collective-permute-start = (bf16[128,1024]{1,0:T(8,128)(2,1)S(1)}, bf16[128,1024]{1,0:T(8,128)(2,1)S(1)}, u32[]{:S(2)}, u32[]{:S(2)}) collective-permute-start(bf16[128,1024]{1,0:T(8,128)(2,1)S(1)} %pad_maximum_fusion), channel_id=1, source_target_pairs={{0,1},{1,2},{2,3},{3,4},{4,5},{5,6},{6,7},{7,8},{8,9},{9,10},{10,1... | collective-permute-start | bytes 786440 | tf_op jit(solution)/shard_map/ppermute | solution.py:126
  10.8 2.4 %copy-start.3 = (s32[27,3072]{1,0:T(8,128)S(1)}, s32[27,3072]{1,0:T(8,128)}, u32[]{:S(2)}) copy-start(s32[27,3072]{1,0:T(8,128)} %param.8) | copy-start | bytes 995332
  10.8 5.7 %collective-permute-start.1 = (bf16[128,1024]{1,0:T(8,128)(2,1)S(1)}, bf16[128,1024]{1,0:T(8,128)(2,1)S(1)}, u32[]{:S(2)}, u32[]{:S(2)}) collective-permute-start(bf16[128,1024]{1,0:T(8,128)(2,1)S(1)} %pad_maximum_fusion.1), channel_id=1, source_target_pairs={{1,0},{2,1},{3,2},{4,3},{5,4},{6,5},{7,6},{8,7},{9,8},{10,9},{11,1... | collective-permute-start | bytes 786440 | tf_op jit(solution)/shard_map/ppermute | solution.py:127
  13.4 3.1 %copy-start = (bf16[64,3072]{1,0:T(8,128)(2,1)S(1)}, bf16[64,3072]{1,0:T(8,128)(2,1)}, u32[]{:S(2)}) copy-start(bf16[64,3072]{1,0:T(8,128)(2,1)} %feat.1) | copy-start | bytes 1179652
  13.4 3.1 %copy-start.1 = (bf16[64,3072]{1,0:T(8,128)(2,1)S(1)}, bf16[64,3072]{1,0:T(8,128)(2,1)}, u32[]{:S(2)}) copy-start(bf16[64,3072]{1,0:T(8,128)(2,1)} %cot.1) | copy-start | bytes 1179652
Sparse Core Ops, SparseCore 0:
  65.7 108.7 all-reduce.3

commit v2 on v1

--- a/solution.py
+++ b/solution.py
@@ -17,7 +17,7 @@
     flags, index, filled,
     feat, cot, left, right, stack,
     out_ref, gf_ref, gw_ref,
-    picked, table, block, ups, compact, result,
+    picked, table, block, ups, compact, result, grads,
 ):
     rim_len = RB * BRICK
     wide = 2 * channels
@@ -31,25 +31,23 @@
         cols = slice(b * BRICK, (b + 1) * BRICK)
         fill_table(b * BRICK, left[:, cols])
         fill_table(rim_len + own_len + b * BRICK, right[:, cols])
-    for b in range(bricks):
-        cols = slice(b * BRICK, (b + 1) * BRICK)
-        up = cot[:, cols].astype(jnp.float32)
-        if RB <= b < bricks - RB:
-            up = jnp.where(b - RB < filled[0], up, 0.0)
-        own = jnp.concatenate([feat[:, cols].astype(jnp.float32), up], axis=0)
-        fill_table(rim_len + b * BRICK, own)
     table[pl.ds(none, 8), :] = jnp.zeros((8, wide), jnp.float32)
     result[...] = jnp.zeros_like(result)
-    gw_ref[...] = jnp.zeros_like(gw_ref)
-
-    def note(step, count):
-        for j in range(16):
-            voxel = step * 16 + j
-            picked[count] = voxel
-            count = count + flags[voxel]
+    grads[...] = jnp.zeros_like(grads)
+
+    def prepare(b, count):
+        start = pl.multiple_of(b * BRICK, BRICK)
+        cols = pl.ds(start, BRICK)
+        live = (b < RB) | (b >= bricks - RB) | (b - RB < filled[0])
+        up = jnp.where(live, cot[:, cols].astype(jnp.float32), 0.0)
+        own = jnp.concatenate([feat[:, cols].astype(jnp.float32), up], axis=0)
+        table[pl.ds(start + rim_len, BRICK), :] = own.T
+        for j in range(BRICK):
+            picked[count] = start + j
+            count = count + flags[start + j]
         return count
 
-    count = lax.fori_loop(0, own_len // 16, note, 0)
+    count = lax.fori_loop(0, bricks, prepare, 0)
 
     def pad(i, _):
         picked[count + i] = 0
@@ -80,14 +78,22 @@
             cols = slice(k * wide, (k + many) * wide)
             part = block[:, :, cols].reshape(ROWS, many * wide).astype(jnp.bfloat16)
             total += jnp.dot(part, stack[cols, :], preferred_element_type=jnp.float32)
-            grad = jnp.dot(up, part, preferred_element_type=jnp.float32)
-            for m in range(many):
-                gw_ref[k + m] += grad[:, m * wide : m * wide + channels]
+            grads[k // 2, :, : many * wide] += jnp.dot(
+                up, part, preferred_element_type=jnp.float32
+            )
         compact[pl.ds(pl.multiple_of(base, ROWS), ROWS), :] = total
         return _
 
     lax.fori_loop(0, (count + ROWS - 1) // ROWS, visit, 0)
-    gw_ref[...] = gw_ref[...] * factor
+    pairs = (taps + 1) // 2
+    for p in range(pairs):
+        both = grads[p] * factor
+        gw_ref[p * channels : (p + 1) * channels, :] = jnp.concatenate(
+            [both[:, :channels], both[:, wide : wide + channels]], axis=1
+        )
+    spare = gw_ref.shape[0] - pairs * channels
+    if spare:
+        gw_ref[pairs * channels :, :] = jnp.zeros((spare, wide), jnp.float32)
 
     def place(step, _):
         for j in range(8):
@@ -110,6 +116,98 @@
             both = jnp.where(b - RB < filled[0], both, 0.0)
         out_ref[:, cols] = both[:channels].astype(jnp.bfloat16)
         gf_ref[:, cols] = both[channels:].astype(jnp.bfloat16)
+
+
+def sum_kernel(count, taps, channels, part, out, peer, mine, inbox, final, *sems):
+    half = count // 2
+    me = lax.axis_index("gx")
+    chip, core = me // 2, me % 2
+    twin = me + 1 - 2 * core
+    near_send, near_recv, far_send, far_recv, all_send, all_recv, end_send, end_recv = sems
+
+    def other(d):
+        return ((chip + d) % half) * 2 + core
+
+    def send(src, dst, send_sem, recv_sem, target):
+        return pltpu.make_async_remote_copy(
+            src_ref=src,
+            dst_ref=dst,
+            send_sem=send_sem,
+            recv_sem=recv_sem,
+            device_id={"gx": target},
+            device_id_type=pl.DeviceIdType.MESH,
+        )
+
+    barrier = pltpu.get_barrier_semaphore()
+    for target in [twin] + [other(d) for d in range(1, half)]:
+        pl.semaphore_signal(
+            barrier, inc=1, device_id={"gx": target}, device_id_type=pl.DeviceIdType.MESH
+        )
+    pl.semaphore_wait(barrier, half)
+
+    order = list(range(1, half)) + [0]
+    near = {}
+    for d in order:
+        t = (chip + d) % half
+        near[d] = send(
+            part.at[(1 - core) * half + t], peer.at[d], near_send.at[d], near_recv.at[d], twin
+        )
+        near[d].start()
+    far = {}
+    for d in order:
+        t = (chip + d) % half
+        near[d].wait_recv()
+        mine[d] = part[core * half + t] + peer[d]
+        if d:
+            far[d] = send(mine.at[d], inbox.at[d], far_send.at[d], far_recv.at[d], other(d))
+            far[d].start()
+    total = mine[0]
+    for d in range(1, half):
+        far[d].wait_recv()
+        total = total + inbox[d]
+    slot = core * half + chip
+    final[slot] = total
+    ends = [send(final.at[slot], final.at[slot], end_send.at[0], end_recv.at[0], twin)]
+    spread = {}
+    for d in range(1, half):
+        spread[d] = send(final.at[slot], final.at[slot], all_send.at[d], all_recv.at[d], other(d))
+        spread[d].start()
+    ends[0].start()
+    for d in range(1, half):
+        got = core * half + (chip + half - d) % half
+        send(final.at[got], final.at[got], all_send.at[d], all_recv.at[d], twin).wait_recv()
+        ends.append(send(final.at[got], final.at[got], end_send.at[d], end_recv.at[d], twin))
+        ends[d].start()
+    for d in range(half):
+        ends[d].wait_recv()
+    whole = final[...].reshape(-1, 2 * channels)
+    for k in range(taps):
+        tile = whole[k // 2 * channels : (k // 2 + 1) * channels]
+        out[k] = tile[:, k % 2 * channels : (k % 2 + 1) * channels]
+    for d in range(half):
+        near[d].wait_send()
+        ends[d].wait_send()
+        if d:
+            far[d].wait_send()
+            spread[d].wait_send()
+
+
+def sum_over_gx(part, taps, channels):
+    count, share, wide = part.shape
+    half = count // 2
+    vmem = pl.BlockSpec(memory_space=pltpu.VMEM)
+    return pl.pallas_call(
+        functools.partial(sum_kernel, count, taps, channels),
+        out_shape=jax.ShapeDtypeStruct((taps, channels, channels), jnp.float32),
+        in_specs=[vmem],
+        out_specs=vmem,
+        scratch_shapes=[pltpu.VMEM((half, share, wide), jnp.float32)] * 3
+        + [pltpu.VMEM((count, share, wide), jnp.float32)]
+        + [pltpu.SemaphoreType.DMA((half,))] * 8,
+        compiler_params=pltpu.CompilerParams(
+            collective_id=0, has_side_effects=True, vmem_limit_bytes=16 * 1024 * 1024
+        ),
+    )(part)
 
 
 def per_device(features, cotangent, weights, kernel_map, interior_bricks):
@@ -126,6 +224,8 @@
     left = lax.ppermute(tail, "gx", [(i, i + 1) for i in range(count - 1)])
     right = lax.ppermute(head, "gx", [(i + 1, i) for i in range(count - 1)])
     flags = jnp.any(kernel_map != none, axis=0).astype(jnp.int32)
+    share = -(-((taps + 1) // 2 * channels) // (8 * count)) * 8
+    rows = count * share
     zero = jnp.zeros_like(weights)
     stack = jnp.concatenate(
         [
@@ -141,7 +241,7 @@
         out_shape=(
             jax.ShapeDtypeStruct((channels, own_len), jnp.bfloat16),
             jax.ShapeDtypeStruct((channels, own_len), jnp.bfloat16),
-            jax.ShapeDtypeStruct((taps, channels, channels), jnp.float32),
+            jax.ShapeDtypeStruct((rows, wide), jnp.float32),
         ),
         in_specs=[smem] * 3 + [vmem] * 5,
         out_specs=(vmem,) * 3,
@@ -152,10 +252,11 @@
             pltpu.VMEM((ROWS // 8, 8, wide), jnp.float32),
             pltpu.VMEM((own_len, wide), jnp.float32),
             pltpu.VMEM((own_len, wide), jnp.float32),
+            pltpu.VMEM(((taps + 1) // 2, channels, 2 * wide), jnp.float32),
         ],
         compiler_params=pltpu.CompilerParams(vmem_limit_bytes=48 * 1024 * 1024),
     )(flags, kernel_map.reshape(-1), interior_bricks, features, cotangent, left, right, stack)
-    grad_weights = lax.psum(partial, "gx")
+    grad_weights = sum_over_gx(partial.reshape(count, rows // count, wide), taps, channels)
     return output, grad_features, grad_weights
 
 

time: 185 us -> 96.9 us (0.52)
  waiting for transfers between devices: 112 us -> 2.82 us
  Pallas kernels: 49.1 us -> 85.6 us
  between operations: 14.8 us -> 1.42 us
    psum x1 -> x0, waiting for transfers between devices: 109 us -> none  [per_device(): grad_weights = lax.psum(partial, 'gx')]
    pallas_call x0 -> x1, Pallas kernels: none -> 36 us  [sum_over_gx(): pl.pallas_call(functools.partial(sum_kernel, count, taps, channels), out_...]
  transfers between devices with their start and end apart: 3 -> 2, of which waited for: 2 -> 1; matrix products, arithmetic and copies ran while one was open for 0% -> 1% of each run, Pallas kernels for 0% -> 0%
where the time goes in v2:
time: 96.9 us; the launch traced here: 96.5 us
  Pallas kernels  85.6 us (88%)
  starting transfers between devices  3.8 us (4%)
  waiting for transfers between devices  2.82 us (3%)
  local copies, waits for them, and re-layouts  2.49 us (3%)
  between operations  1.42 us (1%)
    pallas_call x1, Pallas kernels, per_device(): pl.pallas_call(functools.partial(gather_kernel, taps, channels, own_len,...  49.6 us
    pallas_call x1, Pallas kernels, sum_over_gx(): pl.pallas_call(functools.partial(sum_kernel, count, taps, channels), out_...  36 us
    ppermute x1, waiting for transfers between devices, per_device(): right = lax.ppermute(head, 'gx', [(i + 1, i) for i in range(count - 1)])  2.82 us
    ppermute x1, starting transfers between devices, per_device(): left = lax.ppermute(tail, 'gx', [(i, i + 1) for i in range(count - 1)])  2.37 us
  transfers between devices with their start and end apart: 2, of which 1 were waited for; matrix products, arithmetic and copies ran while one was open for 1% of the time, Pallas kernels for 0%

profile of v2, /device:TPU:0, one launch (start us, length us, event | category | flops | bytes accessed | tf_op | source)
XLA Modules:
  0.0 96.5 jit_solution(17558940238239535238)
XLA Ops:
  0.6 0.0 copy-start.2
  0.6 1.2 %fusion.3 = (bf16[64,1024]{1,0:T(8,128)(2,1)S(1)}, bf16[64,1024]{1,0:T(8,128)(2,1)S(1)}, bf16[64,1024]{1,0:T(8,128)(2,1)S(1)}, bf16[64,1024]{1,0:T(8,128)(2,1)S(1)}) fusion(bf16[64,3072]{1,0:T(8,128)(2,1)} %feat.1, bf16[64,3072]{1,0:T(8,128)(2,1)} %cot.1), kind=kLoop, calls=%fused_computation.8 | loop fusion | bytes 1048576 | tf_op jit(solution)/shard_map/slice | solution.py:223
  1.9 2.4 %collective-permute-start = (bf16[128,1024]{1,0:T(8,128)(2,1)S(1)}, bf16[128,1024]{1,0:T(8,128)(2,1)S(1)}, u32[]{:S(2)}, u32[]{:S(2)}) collective-permute-start(bf16[128,1024]{1,0:T(8,128)(2,1)S(1)} %pad_maximum_fusion), channel_id=1, source_target_pairs={{0,1},{1,2},{2,3},{3,4},{4,5},{5,6},{6,7},{7,8},{8,9},{9,10},{10,1... | collective-permute-start | bytes 786440 | tf_op jit(solution)/shard_map/ppermute | solution.py:224
  4.3 0.0 copy-start.3
  4.3 1.4 %collective-permute-start.1 = (bf16[128,1024]{1,0:T(8,128)(2,1)S(1)}, bf16[128,1024]{1,0:T(8,128)(2,1)S(1)}, u32[]{:S(2)}, u32[]{:S(2)}) collective-permute-start(bf16[128,1024]{1,0:T(8,128)(2,1)S(1)} %pad_maximum_fusion.1), channel_id=1, source_target_pairs={{1,0},{2,1},{3,2},{4,3},{5,4},{6,5},{7,6},{8,7},{9,8},{10,9},{11,1... | collective-permute-start | bytes 786440 | tf_op jit(solution)/shard_map/ppermute | solution.py:225
  5.7 0.0 copy-done.2
  5.8 0.3 copy.8
  6.7 0.0 copy-done.3
  6.7 0.1 reshape.15.index
  6.8 0.1 compare_reduce_fusion
  6.8 0.0 copy-start
  6.9 0.0 copy-start.1
  6.9 0.3 fusion.2
  7.1 0.0 collective-permute-done.left
  7.1 2.8 %collective-permute-done.1.right = bf16[128,1024]{1,0:T(8,128)(2,1)S(1)} collective-permute-done((bf16[128,1024]{1,0:T(8,128)(2,1)S(1)}, bf16[128,1024]{1,0:T(8,128)(2,1)S(1)}, u32[]{:S(2)}, u32[]{:S(2)}) %collective-permute-start.1) | collective-permute-done | bytes 262176 | tf_op jit(solution)/shard_map/ppermute | solution.py:225
  10.0 0.0 copy-done
  10.0 0.0 copy-done.1
  10.0 49.6 %shard_map.76 = (bf16[64,3072]{1,0:T(8,128)(2,1)}, bf16[64,3072]{1,0:T(8,128)(2,1)}, f32[896,128]{1,0:T(8,128)S(1)}) custom-call(s32[3072]{0:T(1024)S(1)} %convert_element_type.3.flags, s32[82944]{0:T(1024)S(1)} %reshape.15.index, s32[1]{0:T(128)S(6)} %copy.10.filled, bf16[64,3072]{1,0:T(8,128)(2,1)S(1)} %copy-done, bf16[64,3072]{1,0:T(8,128)(2,1)S(1)} %copy-done.1, ...), custom_call_target="tpu_custom_call" | custom-call | tf_op jit(solution)/shard_map/pallas_call | solution.py:239
  59.6 36.0 %shard_map.77 = f32[27,64,64]{2,1,0:T(8,128)S(1)} custom-call(f32[16,56,128]{2,1,0:T(8,128)S(1)} %bitcast.4), custom_call_target="tpu_custom_call" | custom-call | tf_op jit(solution)/shard_map/pallas_call | solution.py:199
  95.6 0.9 copy.11
  (4 shorter events, 0.1 us)
Async XLA Ops:
  0.6 5.1 %copy-start.2 = (bf16[27,64,64]{2,1,0:T(8,128)(2,1)S(1)}, bf16[27,64,64]{2,1,0:T(8,128)(2,1)}, u32[]{:S(2)}) copy-start(bf16[27,64,64]{2,1,0:T(8,128)(2,1)} %param.7) | copy-start | bytes 663556
  1.9 5.3 %collective-permute-start = (bf16[128,1024]{1,0:T(8,128)(2,1)S(1)}, bf16[128,1024]{1,0:T(8,128)(2,1)S(1)}, u32[]{:S(2)}, u32[]{:S(2)}) collective-permute-start(bf16[128,1024]{1,0:T(8,128)(2,1)S(1)} %pad_maximum_fusion), channel_id=1, source_target_pairs={{0,1},{1,2},{2,3},{3,4},{4,5},{5,6},{6,7},{7,8},{8,9},{9,10},{10,1... | collective-permute-start | bytes 786440 | tf_op jit(solution)/shard_map/ppermute | solution.py:224
  4.3 2.4 %copy-start.3 = (s32[27,3072]{1,0:T(8,128)S(1)}, s32[27,3072]{1,0:T(8,128)}, u32[]{:S(2)}) copy-start(s32[27,3072]{1,0:T(8,128)} %param.8) | copy-start | bytes 995332
  4.3 5.7 %collective-permute-start.1 = (bf16[128,1024]{1,0:T(8,128)(2,1)S(1)}, bf16[128,1024]{1,0:T(8,128)(2,1)S(1)}, u32[]{:S(2)}, u32[]{:S(2)}) collective-permute-start(bf16[128,1024]{1,0:T(8,128)(2,1)S(1)} %pad_maximum_fusion.1), channel_id=1, source_target_pairs={{1,0},{2,1},{3,2},{4,3},{5,4},{6,5},{7,6},{8,7},{9,8},{10,9},{11,1... | collective-permute-start | bytes 786440 | tf_op jit(solution)/shard_map/ppermute | solution.py:225
  6.8 3.1 %copy-start = (bf16[64,3072]{1,0:T(8,128)(2,1)S(1)}, bf16[64,3072]{1,0:T(8,128)(2,1)}, u32[]{:S(2)}) copy-start(bf16[64,3072]{1,0:T(8,128)(2,1)} %feat.1) | copy-start | bytes 1179652
  6.9 3.1 %copy-start.1 = (bf16[64,3072]{1,0:T(8,128)(2,1)S(1)}, bf16[64,3072]{1,0:T(8,128)(2,1)}, u32[]{:S(2)}) copy-start(bf16[64,3072]{1,0:T(8,128)(2,1)} %cot.1) | copy-start | bytes 1179652

commit v3 on v2

--- a/solution.py
+++ b/solution.py
@@ -12,12 +12,31 @@
 ROWS = 256
 
 
+def list_kernel(own_len, flags, picked, many):
+    def note(step, count):
+        start = step * BRICK
+        for j in range(BRICK):
+            picked[count] = start + j
+            count = count + flags[start + j]
+        return count
+
+    count = lax.fori_loop(0, own_len // BRICK, note, 0)
+
+    def pad(step, _):
+        for j in range(32):
+            picked[count + step * 32 + j] = 0
+        return _
+
+    lax.fori_loop(0, ROWS // 32, pad, 0)
+    many[0] = count
+
+
 def gather_kernel(
     taps, channels, own_len, factor,
-    flags, index, filled,
+    picked, many, index, filled,
     feat, cot, left, right, stack,
     out_ref, gf_ref, gw_ref,
-    picked, table, block, ups, compact, result, grads,
+    table, block, ups, compact, result, grads,
 ):
     rim_len = RB * BRICK
     wide = 2 * channels
@@ -35,35 +54,30 @@
     result[...] = jnp.zeros_like(result)
     grads[...] = jnp.zeros_like(grads)
 
-    def prepare(b, count):
+    def prepare(b, _):
         start = pl.multiple_of(b * BRICK, BRICK)
         cols = pl.ds(start, BRICK)
         live = (b < RB) | (b >= bricks - RB) | (b - RB < filled[0])
         up = jnp.where(live, cot[:, cols].astype(jnp.float32), 0.0)
         own = jnp.concatenate([feat[:, cols].astype(jnp.float32), up], axis=0)
         table[pl.ds(start + rim_len, BRICK), :] = own.T
-        for j in range(BRICK):
-            picked[count] = start + j
-            count = count + flags[start + j]
-        return count
-
-    count = lax.fori_loop(0, bricks, prepare, 0)
-
-    def pad(i, _):
-        picked[count + i] = 0
-        return _
-
-    lax.fori_loop(0, ROWS, pad, 0)
+        return _
+
+    lax.fori_loop(0, bricks, prepare, 0)
+    count = many[0]
 
     def visit(blk, _):
         base = blk * ROWS
 
         def fetch(step, _):
+            sources = []
             for j in range(8):
                 voxel = picked[base + step * 8 + j]
                 ups[step, j : j + 1, :] = table[pl.ds(voxel + rim_len, 1), :]
-                for k in range(taps):
-                    source = index[k * own_len + voxel]
+                sources.append(index.at[pl.ds(voxel, (taps - 1) * own_len + 1)])
+            for k in range(taps):
+                for j in range(8):
+                    source = sources[j][k * own_len]
                     block[step, j : j + 1, k * wide : (k + 1) * wide] = table[pl.ds(source, 1), :]
             return _
 
@@ -74,11 +88,11 @@
         up = up.T[channels:].astype(jnp.bfloat16)
         total = jnp.zeros((ROWS, wide), jnp.float32)
         for k in range(0, taps, 2):
-            many = min(2, taps - k)
-            cols = slice(k * wide, (k + many) * wide)
-            part = block[:, :, cols].reshape(ROWS, many * wide).astype(jnp.bfloat16)
+            both = min(2, taps - k)
+            cols = slice(k * wide, (k + both) * wide)
+            part = block[:, :, cols].reshape(ROWS, both * wide).astype(jnp.bfloat16)
             total += jnp.dot(part, stack[cols, :], preferred_element_type=jnp.float32)
-            grads[k // 2, :, : many * wide] += jnp.dot(
+            grads[k // 2, :, : both * wide] += jnp.dot(
                 up, part, preferred_element_type=jnp.float32
             )
         compact[pl.ds(pl.multiple_of(base, ROWS), ROWS), :] = total
@@ -236,6 +250,18 @@
     ).reshape(taps * wide, wide)
     smem = pl.BlockSpec(memory_space=pltpu.SMEM)
     vmem = pl.BlockSpec(memory_space=pltpu.VMEM)
+    picked, many = pl.pallas_call(
+        functools.partial(list_kernel, own_len),
+        out_shape=(
+            jax.ShapeDtypeStruct((own_len + ROWS,), jnp.int32),
+            jax.ShapeDtypeStruct((1,), jnp.int32),
+        ),
+        in_specs=[smem],
+        out_specs=(smem, smem),
+        cost_estimate=pl.CostEstimate(
+            flops=own_len * 2048, bytes_accessed=own_len * 2048, transcendentals=0
+        ),
+    )(flags)
     output, grad_features, partial = pl.pallas_call(
         functools.partial(gather_kernel, taps, channels, own_len, factor),
         out_shape=(
@@ -243,10 +269,9 @@
             jax.ShapeDtypeStruct((channels, own_len), jnp.bfloat16),
             jax.ShapeDtypeStruct((rows, wide), jnp.float32),
         ),
-        in_specs=[smem] * 3 + [vmem] * 5,
+        in_specs=[smem] * 4 + [vmem] * 5,
         out_specs=(vmem,) * 3,
         scratch_shapes=[
-            pltpu.SMEM((own_len + ROWS,), jnp.int32),
             pltpu.VMEM((none + 8, wide), jnp.float32),
             pltpu.VMEM((ROWS // 8, 8, taps * wide), jnp.float32),
             pltpu.VMEM((ROWS // 8, 8, wide), jnp.float32),
@@ -255,7 +280,7 @@
             pltpu.VMEM(((taps + 1) // 2, channels, 2 * wide), jnp.float32),
         ],
         compiler_params=pltpu.CompilerParams(vmem_limit_bytes=48 * 1024 * 1024),
-    )(flags, kernel_map.reshape(-1), interior_bricks, features, cotangent, left, right, stack)
+    )(picked, many, kernel_map.reshape(-1), interior_bricks, features, cotangent, left, right, stack)
     grad_weights = sum_over_gx(partial.reshape(count, rows // count, wide), taps, channels)
     return output, grad_features, grad_weights
 

time: 96.9 us -> 85 us (0.88)
  the two profiles are of different devices: /device:TPU:0 before, /device:TPU:27 now
where the time goes in v3:
time: 85 us; the launch traced here: 84.9 us
  Pallas kernels  73.5 us (86%)
  starting transfers between devices  5.76 us (7%)
  local copies, waits for them, and re-layouts  3.29 us (4%)
  between operations  1.44 us (2%)
  other arithmetic  0.96 us (1%)
    pallas_call x1, Pallas kernels, per_device(): pl.pallas_call(functools.partial(gather_kernel, taps, channels, own_len,...  37.9 us
    pallas_call x1, Pallas kernels, sum_over_gx(): pl.pallas_call(functools.partial(sum_kernel, count, taps, channels), out_...  29.7 us
    pallas_call x1, Pallas kernels, per_device(): pl.pallas_call(functools.partial(list_kernel, own_len), out_shape=(jax.Sh...  5.93 us
    ppermute x1, starting transfers between devices, per_device(): left = lax.ppermute(tail, 'gx', [(i, i + 1) for i in range(count - 1)])  3.71 us
    ppermute x1, starting transfers between devices, per_device(): right = lax.ppermute(head, 'gx', [(i + 1, i) for i in range(count - 1)])  2.05 us
    unnamed x12, local copies, waits for them, and re-layouts  2.02 us
  transfers between devices with their start and end apart: 2, of which 0 were waited for; matrix products, arithmetic and copies ran while one was open for 2% of the time, Pallas kernels for 7%

profile of v3, /device:TPU:27, one launch (start us, length us, event | category | flops | bytes accessed | tf_op | source)
XLA Modules:
  0.0 84.9 jit_solution(15707787053495316667)
XLA Ops:
  0.6 0.0 copy-start.3
  0.6 1.2 %fusion.3 = (bf16[64,1024]{1,0:T(8,128)(2,1)S(1)}, bf16[64,1024]{1,0:T(8,128)(2,1)S(1)}, bf16[64,1024]{1,0:T(8,128)(2,1)S(1)}, bf16[64,1024]{1,0:T(8,128)(2,1)S(1)}) fusion(bf16[64,3072]{1,0:T(8,128)(2,1)} %feat.1, bf16[64,3072]{1,0:T(8,128)(2,1)} %cot.1), kind=kLoop, calls=%fused_computation.8 | loop fusion | bytes 1048576 | tf_op jit(solution)/shard_map/slice | solution.py:237
  1.9 3.7 %collective-permute-start = (bf16[128,1024]{1,0:T(8,128)(2,1)S(1)}, bf16[128,1024]{1,0:T(8,128)(2,1)S(1)}, u32[]{:S(2)}, u32[]{:S(2)}) collective-permute-start(bf16[128,1024]{1,0:T(8,128)(2,1)S(1)} %pad_maximum_fusion), channel_id=1, source_target_pairs={{0,1},{1,2},{2,3},{3,4},{4,5},{5,6},{6,7},{7,8},{8,9},{9,10},{10,1... | collective-permute-start | bytes 786440 | tf_op jit(solution)/shard_map/ppermute | solution.py:238
  5.6 0.0 copy-start.4
  5.6 2.1 %collective-permute-start.1 = (bf16[128,1024]{1,0:T(8,128)(2,1)S(1)}, bf16[128,1024]{1,0:T(8,128)(2,1)S(1)}, u32[]{:S(2)}, u32[]{:S(2)}) collective-permute-start(bf16[128,1024]{1,0:T(8,128)(2,1)S(1)} %pad_maximum_fusion.1), channel_id=1, source_target_pairs={{1,0},{2,1},{3,2},{4,3},{5,4},{6,5},{7,6},{8,7},{9,8},{10,9},{11,1... | collective-permute-start | bytes 786440 | tf_op jit(solution)/shard_map/ppermute | solution.py:239
  7.7 0.0 copy-done.3
  7.7 0.3 copy.8
  8.7 0.0 copy-done.4
  8.7 0.1 reshape.15.index
  8.7 0.1 compare_reduce_fusion
  8.8 0.6 convert_element_type.3.flags
  9.4 5.9 %shard_map.76 = (s32[3328]{0:T(1024)}, s32[1]{0:T(128)}) custom-call(s32[3072]{0:T(1024)} %convert_element_type.3.flags), custom_call_target="tpu_custom_call" | custom-call | flops 6291456 | bytes 6291456 | tf_op jit(solution)/shard_map/pallas_call | solution.py:253
  15.3 0.0 copy-start
  15.4 0.0 copy-start.1
  15.4 0.0 copy-start.2
  15.4 0.3 fusion.2
  15.6 0.0 collective-permute-done.left
  15.6 0.0 collective-permute-done.1.right
  15.7 0.7 copy-done
  16.3 0.1 copy-done.1
  16.5 0.0 copy-done.2
  16.5 37.9 %shard_map.77 = (bf16[64,3072]{1,0:T(8,128)(2,1)}, bf16[64,3072]{1,0:T(8,128)(2,1)}, f32[896,128]{1,0:T(8,128)S(1)}) custom-call(s32[3328]{0:T(1024)S(1)} %copy-done.2, s32[1]{0:T(128)} %get-tuple-element.9.many, s32[82944]{0:T(1024)S(1)} %reshape.15.index, s32[1]{0:T(128)S(6)} %copy.10.filled, bf16[64,3072]{1,0:T(8,128)(2,1)S(1)} %copy-done, ...), custom_call_target="tpu_custom_call" | custom-call | tf_op jit(solution)/shard_map/pallas_call | solution.py:265
  54.3 29.7 %shard_map.78 = f32[27,64,64]{2,1,0:T(8,128)S(1)} custom-call(f32[16,56,128]{2,1,0:T(8,128)S(1)} %bitcast.4), custom_call_target="tpu_custom_call" | custom-call | tf_op jit(solution)/shard_map/pallas_call | solution.py:213
  84.0 0.9 %copy.11 = f32[27,64,64]{2,1,0:T(8,128)} copy(f32[27,64,64]{2,1,0:T(8,128)S(1)} %shard_map.78) | data formatting | bytes 884736
  (3 shorter events, 0.1 us)
Async XLA Ops:
  0.6 7.0 %copy-start.3 = (bf16[27,64,64]{2,1,0:T(8,128)(2,1)S(1)}, bf16[27,64,64]{2,1,0:T(8,128)(2,1)}, u32[]{:S(2)}) copy-start(bf16[27,64,64]{2,1,0:T(8,128)(2,1)} %param.7) | copy-start | bytes 663556
  1.9 13.8 %collective-permute-start = (bf16[128,1024]{1,0:T(8,128)(2,1)S(1)}, bf16[128,1024]{1,0:T(8,128)(2,1)S(1)}, u32[]{:S(2)}, u32[]{:S(2)}) collective-permute-start(bf16[128,1024]{1,0:T(8,128)(2,1)S(1)} %pad_maximum_fusion), channel_id=1, source_target_pairs={{0,1},{1,2},{2,3},{3,4},{4,5},{5,6},{6,7},{7,8},{8,9},{9,10},{10,1... | collective-permute-start | bytes 786440 | tf_op jit(solution)/shard_map/ppermute | solution.py:238
  5.6 3.1 %copy-start.4 = (s32[27,3072]{1,0:T(8,128)S(1)}, s32[27,3072]{1,0:T(8,128)}, u32[]{:S(2)}) copy-start(s32[27,3072]{1,0:T(8,128)} %param.8) | copy-start | bytes 995332
  5.6 10.0 %collective-permute-start.1 = (bf16[128,1024]{1,0:T(8,128)(2,1)S(1)}, bf16[128,1024]{1,0:T(8,128)(2,1)S(1)}, u32[]{:S(2)}, u32[]{:S(2)}) collective-permute-start(bf16[128,1024]{1,0:T(8,128)(2,1)S(1)} %pad_maximum_fusion.1), channel_id=1, source_target_pairs={{1,0},{2,1},{3,2},{4,3},{5,4},{6,5},{7,6},{8,7},{9,8},{10,9},{11,1... | collective-permute-start | bytes 786440 | tf_op jit(solution)/shard_map/ppermute | solution.py:239
  15.3 1.0 %copy-start = (bf16[64,3072]{1,0:T(8,128)(2,1)S(1)}, bf16[64,3072]{1,0:T(8,128)(2,1)}, u32[]{:S(2)}) copy-start(bf16[64,3072]{1,0:T(8,128)(2,1)} %feat.1) | copy-start | bytes 1179652
  15.4 1.1 %copy-start.1 = (bf16[64,3072]{1,0:T(8,128)(2,1)S(1)}, bf16[64,3072]{1,0:T(8,128)(2,1)}, u32[]{:S(2)}) copy-start(bf16[64,3072]{1,0:T(8,128)(2,1)} %cot.1) | copy-start | bytes 1179652
  15.4 1.1 %copy-start.2 = (s32[3328]{0:T(1024)S(1)}, s32[3328]{0:T(1024)}, u32[]{:S(2)}) copy-start(s32[3328]{0:T(1024)} %get-tuple-element.8.picked) | copy-start | bytes 39940
